TPU v7x, 512 devices: a whole 4x8x8 slice. The times are simulated.
512 devices in a mesh: seq: 64 (over z_hi, y, core), head: 8 (over z_lo, x).
Axes of the slice: x: 4, y: 8, z: 8 (z_hi: 4, z_lo: 2; z = z_hi * 2 + z_lo), core: 2. Of those that a mesh axis runs over, the one named last changes fastest.
Arguments:
- query_feats: bfloat16 [32768, 4096], P('seq', 'head'), may hold values from -16 to 16
- key_feats: bfloat16 [32768, 1024], P('seq', 'head'), may hold values from -7 to 7
- value_feats: bfloat16 [32768, 1024], P('seq', 'head'), may hold values from -6 to 6
- span_class: int32 [32], replicated, may hold values from 1 to 16, as said below
- ramp_width: int32 [32], replicated, may hold values from 32 to 128
- doc_lengths: int32 [16], replicated, may hold values from 1 to 16384, 32768 in all
- out_proj: bfloat16 [4096, 4096], P('seq', 'head'), may hold values from -0.5 to 0.5
Outputs:
- mixed: bfloat16 [32768, 4096], P(('seq', 'head'))
Inputs may be any that keep to these rules, and one draw needn't show every extreme that they name: `span_class`: some head has a span of 16 tiles.
All inputs are finite; a program needn't handle non-finite values.
Results may differ from a plain program's by a relative error of at most 0.014.
Values may be sent and summed in bfloat16 or wider, within the bound.
A program may use at most 64 MiB of HBM per device.

v0:
```python
from functools import partial
import math

import jax
import jax.numpy as jnp
from jax import lax
from jax.sharding import PartitionSpec as P

HD = 128
TILE = 128
BACK = 4


very_low = -1e30


def shifted(block, axis, distance):
    devices = range(lax.axis_size(axis))
    route = [(i - distance, i) for i in devices if i - distance in devices]
    return lax.ppermute(block, axis, route)


def attend(running, key_pair, key_start, context):
    queries, query_pos, doc_start, span_end, ramp_float = context
    top_score, denominator, numerator = running
    tok_rows, kv_count, ratio, head_dim = queries.shape
    key_block = key_pair[0].reshape(tok_rows, kv_count, head_dim)
    value_block = key_pair[1].reshape(tok_rows, kv_count, head_dim)
    scores = jnp.einsum(
        "qgrd,kgd->qgrk", queries, key_block, preferred_element_type=jnp.float32
    ) * (1.0 / math.sqrt(head_dim))
    key_pos = key_start + jnp.arange(tok_rows, dtype=jnp.int32)
    distance = query_pos[:, None] - key_pos[None, :]
    visible = (distance >= 0) & (key_pos[None, :] >= doc_start[:, None])
    weights = jnp.clip(
        (span_end[None, :, :, None] - distance[:, None, None, :].astype(jnp.float32))
        / ramp_float[None, :, :, None],
        0.0,
        1.0,
    )
    weights = jnp.where(visible[:, None, None, :], weights, 0.0)
    limited = jnp.where(weights > 0.0, scores, very_low)
    new_top = jnp.maximum(top_score, jnp.max(limited, axis=3))
    rescale = jnp.exp(top_score - new_top)
    prob_terms = weights * jnp.exp(limited - new_top[:, :, :, None])
    denominator = denominator * rescale + jnp.sum(prob_terms, axis=3)
    numerator = numerator * rescale[:, :, :, None] + jnp.einsum(
        "qgrk,kgd->qgrd",
        prob_terms.astype(jnp.bfloat16),
        value_block,
        preferred_element_type=jnp.float32,
    )
    return (new_top, denominator, numerator)


def unchanged(running):
    return running


def on_device(query_feats, key_feats, value_feats, span_class, ramp_width, doc_lengths, out_proj):
    tok_rows = query_feats.shape[0]
    feat_width = query_feats.shape[1]
    head_count = feat_width // HD
    kv_count = key_feats.shape[1] // HD
    ratio = head_count // kv_count
    seq_index = lax.axis_index("seq")
    head_index = lax.axis_index("head")
    query_pos = seq_index * tok_rows + jnp.arange(tok_rows, dtype=jnp.int32)
    starts = jnp.cumsum(doc_lengths) - doc_lengths
    doc_start = jnp.max(
        jnp.where(starts[None, :] <= query_pos[:, None], starts[None, :], 0), axis=1
    )
    local_span = lax.dynamic_slice_in_dim(span_class, head_index * head_count, head_count)
    local_ramp = lax.dynamic_slice_in_dim(ramp_width, head_index * head_count, head_count)
    span_end = (local_span * TILE).astype(jnp.float32).reshape(kv_count, ratio)
    ramp_float = local_ramp.astype(jnp.float32).reshape(kv_count, ratio)
    context = (
        query_feats.reshape(tok_rows, kv_count, ratio, HD),
        query_pos,
        doc_start,
        span_end,
        ramp_float,
    )
    running = (
        jnp.full((tok_rows, kv_count, ratio), very_low, jnp.float32),
        jnp.zeros((tok_rows, kv_count, ratio), jnp.float32),
        jnp.zeros((tok_rows, kv_count, ratio, HD), jnp.float32),
    )
    own_pair = jnp.stack([key_feats, value_feats])
    running = attend(running, own_pair, seq_index * tok_rows, context)
    reach_most = jnp.max(span_end)
    moving = own_pair
    for offset in range(1, BACK + 1):
        moving = shifted(own_pair, "seq", offset)
        needed = reach_most > float((offset - 1) * tok_rows + 1)
        visit_block = partial(
            attend, key_pair=moving, key_start=(seq_index - offset) * tok_rows, context=context
        )
        running = lax.cond(needed, visit_block, unchanged, running)
    top_score, denominator, numerator = running
    attended = (
        (numerator / denominator[:, :, :, None]).astype(jnp.bfloat16).reshape(tok_rows, feat_width)
    )
    partials = lax.dot_general(
        attended,
        lax.all_gather(out_proj, "seq", axis=0, tiled=True),
        (((1,), (1,)), ((), ())),
        preferred_element_type=jnp.float32,
    )
    mixed_out = lax.psum_scatter(
        partials.astype(jnp.bfloat16), "head", scatter_dimension=0, tiled=True
    )
    return mixed_out


def solution(mesh):
    in_specs = (
        P("seq", "head"),
        P("seq", "head"),
        P("seq", "head"),
        P(),
        P(),
        P(),
        P("seq", "head"),
    )
    out_specs = P(("seq", "head"), None)
    return jax.shard_map(
        on_device, mesh=mesh, in_specs=in_specs, out_specs=out_specs, check_vma=False
    )
```

profile of v0, /device:TPU:1, one launch (start us, length us, event | category | flops | bytes accessed | tf_op | source)
XLA Modules:
  0.0 195.9 jit_solution(2180915210068702400)
XLA Ops:
  6.5 0.7 all-gather.2.cloned.1.call-update
  7.3 1.0 pad_maximum_fusion
  8.3 4.6 %collective-permute-start = (bf16[2,512,128]{2,1,0:T(8,128)(2,1)S(1)}, bf16[2,512,128]{2,1,0:T(8,128)(2,1)S(1)}, u32[]{:S(2)}, u32[]{:S(2)}) collective-permute-start(bf16[2,512,128]{2,1,0:T(8,128)(2,1)S(1)} %pad_maximum_fusion), channel_id=1, source_target_pairs={{0,8},{8,16},{16,24},{24,32},{32,40},{40,48},{48,56},{56,64},{64,7... | collective-permute-start | bytes 786440 | tf_op jit(solution)/shard_map/ppermute | solution.py:20
  12.9 3.2 %collective-permute-start.1 = (bf16[2,512,128]{2,1,0:T(8,128)(2,1)S(1)}, bf16[2,512,128]{2,1,0:T(8,128)(2,1)S(1)}, u32[]{:S(2)}, u32[]{:S(2)}) collective-permute-start(bf16[2,512,128]{2,1,0:T(8,128)(2,1)S(1)} %pad_maximum_fusion), channel_id=1, source_target_pairs={{0,16},{8,24},{16,32},{24,40},{32,48},{40,56},{48,64},{56,72},{64,... | collective-permute-start | bytes 786440 | tf_op jit(solution)/shard_map/ppermute | solution.py:20
  16.1 3.2 %collective-permute-start.2 = (bf16[2,512,128]{2,1,0:T(8,128)(2,1)S(1)}, bf16[2,512,128]{2,1,0:T(8,128)(2,1)S(1)}, u32[]{:S(2)}, u32[]{:S(2)}) collective-permute-start(bf16[2,512,128]{2,1,0:T(8,128)(2,1)S(1)} %pad_maximum_fusion), channel_id=1, source_target_pairs={{0,24},{8,32},{16,40},{24,48},{32,56},{40,64},{48,72},{56,80},{64,... | collective-permute-start | bytes 786440 | tf_op jit(solution)/shard_map/ppermute | solution.py:20
  19.3 4.5 %collective-permute-start.3 = (bf16[2,512,128]{2,1,0:T(8,128)(2,1)S(1)}, bf16[2,512,128]{2,1,0:T(8,128)(2,1)S(1)}, u32[]{:S(2)}, u32[]{:S(2)}) collective-permute-start(bf16[2,512,128]{2,1,0:T(8,128)(2,1)S(1)} %pad_maximum_fusion), channel_id=1, source_target_pairs={{0,32},{8,40},{16,48},{24,56},{32,64},{40,72},{48,80},{56,88},{64,... | collective-permute-start | bytes 786440 | tf_op jit(solution)/shard_map/ppermute | solution.py:20
  23.9 0.7 copy.32
  24.8 0.7 sub.333
  25.4 1.3 fusion.118
  26.8 0.7 dynamic-slice_convert_fusion
  27.6 0.3 fusion.107
  28.1 2.7 %fusion.93 = (f32[512,4]{0,1:T(4,128)S(1)}, f32[512,512,4]{1,0,2:T(8,128)S(1)}) fusion(f32[4]{0:T(128)S(1)} %dynamic-slice_convert_fusion, f32[512,512]{0,1:T(8,128)S(1)} %subtract_convert_fusion.4, f32[4]{0:T(128)S(1)} %get-tuple-element.311, pred[512,512]{0,1:T(8,128)(4,1)S(1)} %fusion.107, bf16[512,128]{1,0:T(8,128)(2,1)} %param.16, ...), kind=kOutput, calls=%fused_computation.117 | convolution fusion | flops 276822016 | bytes 6168608 | tf_op jit(solution)/shard_map/qgrd,kgd->qgrk/dot_general | solution.py:29
  30.8 2.2 %fusion.104 = f32[512,1,4,128]{3,0,2,1:T(8,128)S(1)} fusion(f32[512,4]{0,1:T(4,128)S(1)} %get-tuple-element.324, f32[512,512,4]{1,0,2:T(8,128)S(1)} %get-tuple-element.326, f32[4]{0:T(128)S(1)} %dynamic-slice_convert_fusion, f32[512,512]{0,1:T(8,128)S(1)} %subtract_convert_fusion.4, f32[4]{0:T(128)S(1)} %get-tuple-element.311, ...), kind=kOutput, calls=%fused_computation.126 | convolution fusion | flops 279183360 | bytes 6701088 | tf_op jit(solution)/shard_map/qgrk,kgd->qgrd/dot_general | solution.py:47
  33.1 1.9 fusion.97
  37.8 6.4 %conditional.4 = ((f32[512,1,4]{0,2,1:T(4,128)S(1)}, f32[512,1,4]{0,2,1:T(4,128)S(1)}, f32[512,1,4,128]{3,0,2,1:T(8,128)S(1)})) conditional(s32[]{:T(128)} %convert_element_type.87, (f32[512,1,4]{0,2,1:T(4,128)S(1)}, f32[512,1,4]{0,2,1:T(4,128)S(1)}, f32[512,1,4,128]{3,0,2,1:T(8,128)S(1)}) %tuple.37, (s32[512]{0:T(512)S(1)}, s32[]{:T(128)}, ...), branch_computations={%region_5.6_spmd, %region_6.9_spmd} | conditional | flops 568334848 | bytes 20854852 | solution.py:99
  38.3 1.6 fusion
  39.9 1.9 fusion.4
  41.8 2.4 %fusion.8 = f32[512,1,4,128]{3,0,2,1:T(8,128)S(1)} fusion(f32[512,4]{0,1:T(4,128)S(1)} %bitcast.307, f32[512,512,4]{1,0,2:T(8,128)S(1)} %get-tuple-element.317, f32[4]{0:T(128)S(1)} %get-tuple-element.164, f32[512,512]{0,1:T(8,128)S(1)} %subtract_convert_fusion, f32[4]{0:T(128)S(1)} %get-tuple-element.163, pred[512,512]{0,1:T(8,128)(4,1)S(1)} %fusion.11, ...), kind=kOutput, calls=%fused_computation.11 | convolution fusion | flops 279445504 | bytes 7750656 | tf_op jit(solution)/shard_map/cond/branch_1_fun/qgrk,kgd->qgrd/dot_general | solution.py:47
  44.2 6.6 %conditional.5 = ((f32[512,1,4]{0,2,1:T(4,128)S(1)}, f32[512,1,4]{0,2,1:T(4,128)S(1)}, f32[512,1,4,128]{3,0,2,1:T(8,128)S(1)})) conditional(s32[]{:T(128)} %convert_element_type.86, (f32[512,1,4]{0,2,1:T(4,128)S(1)}, f32[512,1,4]{0,2,1:T(4,128)S(1)}, f32[512,1,4,128]{3,0,2,1:T(8,128)S(1)}) %get-tuple-element.349, (s32[512]{0:T(512)S(1)}, ...), branch_computations={%region_9.10_spmd, %region_10.13_spmd} | conditional | flops 568334848 | bytes 20854852 | solution.py:99
  44.9 1.6 fusion.23
  46.5 1.9 fusion.27
  48.4 2.4 %fusion.31 = f32[512,1,4,128]{3,0,2,1:T(8,128)S(1)} fusion(f32[512,4]{0,1:T(4,128)S(1)} %bitcast.309, f32[512,512,4]{1,0,2:T(8,128)S(1)} %get-tuple-element.319, f32[4]{0:T(128)S(1)} %get-tuple-element.174, f32[512,512]{0,1:T(8,128)S(1)} %subtract_convert_fusion.1, f32[4]{0:T(128)S(1)} %get-tuple-element.173, pred[512,512]{0,1:T(8,128)(4,1)S(1)} %fusion.34, ...), kind=kOutput, calls=%fused_computation.39 | convolution fusion | flops 279445504 | bytes 7750656 | tf_op jit(solution)/shard_map/cond/branch_1_fun/qgrk,kgd->qgrd/dot_general | solution.py:47
  50.8 6.4 %conditional.6 = ((f32[512,1,4]{0,2,1:T(4,128)S(1)}, f32[512,1,4]{0,2,1:T(4,128)S(1)}, f32[512,1,4,128]{3,0,2,1:T(8,128)S(1)})) conditional(s32[]{:T(128)} %convert_element_type.85, (f32[512,1,4]{0,2,1:T(4,128)S(1)}, f32[512,1,4]{0,2,1:T(4,128)S(1)}, f32[512,1,4,128]{3,0,2,1:T(8,128)S(1)}) %get-tuple-element.350, (s32[512]{0:T(512)S(1)}, ...), branch_computations={%region_13.14_spmd, %region_14.17_spmd} | conditional | flops 568334848 | bytes 20854876 | solution.py:99
  51.0 0.3 fusion.57
  51.3 1.6 fusion.46
  52.9 1.9 fusion.50
  54.9 2.4 %fusion.54 = f32[512,1,4,128]{3,0,2,1:T(8,128)S(1)} fusion(f32[512,4]{0,1:T(4,128)S(1)} %bitcast.311, f32[512,512,4]{1,0,2:T(8,128)S(1)} %get-tuple-element.321, f32[4]{0:T(128)S(1)} %get-tuple-element.184, f32[512,512]{0,1:T(8,128)S(1)} %subtract_convert_fusion.2, f32[4]{0:T(128)S(1)} %get-tuple-element.183, pred[512,512]{0,1:T(8,128)(4,1)S(1)} %fusion.57, ...), kind=kOutput, calls=%fused_computation.67 | convolution fusion | flops 279445504 | bytes 7750656 | tf_op jit(solution)/shard_map/cond/branch_1_fun/qgrk,kgd->qgrd/dot_general | solution.py:47
  57.2 0.6 conditional.7
  57.3 0.3 copy.46
  58.0 70.6 %all-gather.2.cloned.1.call-done = bf16[4096,512]{1,0:T(8,128)(2,1)} async-done(((bf16[64,512]{1,0:T(8,128)(2,1)}), bf16[4096,512]{1,0:T(8,128)(2,1)}) %all-gather.2.cloned.1.call-update) | async-done | bytes 4194320 | tf_op jit(solution)/shard_map/all_gather | solution.py:106
  128.6 6.6 %convolution_convert_fusion = bf16[512,4096]{1,0:T(8,128)(2,1)} fusion(bf16[512,512]{0,1:T(8,128)(2,1)S(1)} %bitcast.300, bf16[4096,512]{1,0:T(8,128)(2,1)} %all-gather.2.cloned.1.call-done), kind=kOutput, calls=%fused_computation.113 | convolution fusion | flops 2149580800 | bytes 8912896 | tf_op jit(solution)/shard_map/dot_general | solution.py:104
  135.2 53.9 %reduce-scatter.2.cloned.1.call-done = bf16[64,4096]{1,0:T(8,128)(2,1)} async-done(((bf16[512,4096]{1,0:T(8,128)(2,1)}), bf16[64,4096]{1,0:T(8,128)(2,1)}) %reduce-scatter.2.cloned.1.call-update) | async-done | bytes 524304 | tf_op jit(solution)/shard_map/reduce_scatter | solution.py:110
  (37 shorter events, 2.0 us)
Async XLA Ops:
  6.5 122.1 %all-gather.2.cloned.1.call-start = ((), (), s32[]{:S(2)}) async-start(), calls=%async_computation.1 | async-start | bytes 4259840 | tf_op jit(solution)/shard_map/all_gather | solution.py:106
  7.3 181.8 %reduce-scatter.2.cloned.1.call-start = ((), (), s32[]{:S(2)}) async-start(), calls=%async_computation.2 | async-start | bytes 4718592 | tf_op jit(solution)/shard_map/reduce_scatter | solution.py:110
  8.3 29.5 %collective-permute-start = (bf16[2,512,128]{2,1,0:T(8,128)(2,1)S(1)}, bf16[2,512,128]{2,1,0:T(8,128)(2,1)S(1)}, u32[]{:S(2)}, u32[]{:S(2)}) collective-permute-start(bf16[2,512,128]{2,1,0:T(8,128)(2,1)S(1)} %pad_maximum_fusion), channel_id=1, source_target_pairs={{0,8},{8,16},{16,24},{24,32},{32,40},{40,48},{48,56},{56,64},{64,7... | collective-permute-start | bytes 786440 | tf_op jit(solution)/shard_map/ppermute | solution.py:20
  12.9 31.3 %collective-permute-start.1 = (bf16[2,512,128]{2,1,0:T(8,128)(2,1)S(1)}, bf16[2,512,128]{2,1,0:T(8,128)(2,1)S(1)}, u32[]{:S(2)}, u32[]{:S(2)}) collective-permute-start(bf16[2,512,128]{2,1,0:T(8,128)(2,1)S(1)} %pad_maximum_fusion), channel_id=1, source_target_pairs={{0,16},{8,24},{16,32},{24,40},{32,48},{40,56},{48,64},{56,72},{64,... | collective-permute-start | bytes 786440 | tf_op jit(solution)/shard_map/ppermute | solution.py:20
  16.1 34.7 %collective-permute-start.2 = (bf16[2,512,128]{2,1,0:T(8,128)(2,1)S(1)}, bf16[2,512,128]{2,1,0:T(8,128)(2,1)S(1)}, u32[]{:S(2)}, u32[]{:S(2)}) collective-permute-start(bf16[2,512,128]{2,1,0:T(8,128)(2,1)S(1)} %pad_maximum_fusion), channel_id=1, source_target_pairs={{0,24},{8,32},{16,40},{24,48},{32,56},{40,64},{48,72},{56,80},{64,... | collective-permute-start | bytes 786440 | tf_op jit(solution)/shard_map/ppermute | solution.py:20
  19.3 37.9 %collective-permute-start.3 = (bf16[2,512,128]{2,1,0:T(8,128)(2,1)S(1)}, bf16[2,512,128]{2,1,0:T(8,128)(2,1)S(1)}, u32[]{:S(2)}, u32[]{:S(2)}) collective-permute-start(bf16[2,512,128]{2,1,0:T(8,128)(2,1)S(1)} %pad_maximum_fusion), channel_id=1, source_target_pairs={{0,32},{8,40},{16,48},{24,56},{32,64},{40,72},{48,80},{56,88},{64,... | collective-permute-start | bytes 786440 | tf_op jit(solution)/shard_map/ppermute | solution.py:20
  28.1 2.8 %copy-start.1 = (bf16[512,128]{1,0:T(8,128)(2,1)S(1)}, bf16[512,128]{1,0:T(8,128)(2,1)}, u32[]{:S(2)}) copy-start(bf16[512,128]{1,0:T(8,128)(2,1)} %param.17) | copy-start | bytes 393220
  33.1 1.9 copy-start
Sparse Core Ops, SparseCore 0:
  10.7 117.8 all-gather.1
  135.3 53.6 reduce-scatter.1
where the time goes:
time: 196 us
  waiting for transfers between devices  125 us (64%)
  matrix products  23.4 us (12%)
  between operations  16.2 us (8%)
  starting transfers between devices  15.6 us (8%)
  other arithmetic  13.5 us (7%)
    all_gather x1, waiting for transfers between devices, on_device(): lax.all_gather(out_proj, 'seq', axis=0, tiled=True)  70.6 us
    reduce_scatter x1, waiting for transfers between devices, on_device(): lax.psum_scatter(partials.astype(jnp.bfloat16), 'head', scatter_dimension...  53.9 us
    ppermute x4, starting transfers between devices, shifted(): return lax.ppermute(block, axis, route)  15.6 us
    dot_general x4, matrix products, attend(): jnp.einsum('qgrk,kgd->qgrd', prob_terms.astype(jnp.bfloat16), value_block...  9.32 us
    dot_general x4, matrix products, attend(): jnp.einsum('qgrd,kgd->qgrk', queries, key_block, preferred_element_type=j...  7.55 us
    reduce_sum x4, other arithmetic, attend(): denominator = denominator * rescale + jnp.sum(prob_terms, axis=3)  7.53 us
    dot_general x1, matrix products, on_device(): lax.dot_general(attended, lax.all_gather(out_proj, 'seq', axis=0, tiled=T...  6.56 us
  transfers between devices with their start and end apart: 6, of which 2 were waited for; matrix products, arithmetic and copies ran while one was open for 16% of the time, Pallas kernels for 0%

commit v1 on v0

v1 whole, which is shorter than its diff:
```python
import math

import jax
import jax.numpy as jnp
from jax import lax
from jax.experimental import pallas as pl
from jax.experimental.pallas import tpu as pltpu
from jax.sharding import PartitionSpec as P

HD = 128
TILE = 128
HEADS = 4
TOK = 512
FEAT = HEADS * HD
NZ, NY, NX = 4, 8, 4
NDOCS = 16
ROWS = 64
PLUS, MINUS = 3, 4
COLS = 512
LOW = -1e30
MESH = pl.DeviceIdType.MESH
NT = (((1,), (1,)), ((), ()))
SCALE = math.log2(math.e) / math.sqrt(HD)


def kernel(q_ref, k_ref, v_ref, w_ref, span_ref, ramp_ref, doc_ref, out_ref,
           kbuf, vbuf, qx, kf, btab, s_scr, p_scr, m_scr, acc, att, wg, part,
           far, near, zout, zin,
           kv_send, kv_recv, z_send, z_recv, p_send, p_recv, m_send, m_recv,
           s_send, s_recv, a_send, a_recv, far_send, far_recv, near_send, near_recv,
           zx_send, zx_recv):
    seq = lax.axis_index("seq")
    head = lax.axis_index("head")
    core = lax.rem(seq, 2)
    y = lax.rem(seq // 2, NY)
    zh = seq // (2 * NY)
    x = lax.rem(head, NX)
    zl = head // NX
    half = zh // 2
    n_seq = 2 * NY * NZ

    def at(zh_, y_, c_, zl_, x_):
        return ((zh_ * NY + y_) * 2 + c_, zl_ * NX + x_)

    after = (lax.rem(seq + 2, n_seq), head)
    before = (lax.rem(seq + n_seq - 2, n_seq), head)
    sibling = at(zh, y, 1 - core, zl, x)
    y_up = at(zh, lax.rem(y + 1, NY), core, zl, x)
    y_down = at(zh, lax.rem(y + NY - 1, NY), core, zl, x)
    xr, xl = lax.rem(x + 1, NX), lax.rem(x + NX - 1, NX)
    xo = lax.rem(x + 2, NX)
    x_up = at(zh, y, core, zl, xr)
    x_down = at(zh, y, core, zl, xl)
    partner = at(zh, y, core, 1 - zl, x)

    barrier = pltpu.get_barrier_semaphore()
    greet = [after, before, sibling, y_up, y_down, x_up, x_down, partner]
    for j in range(1, NZ):
        for b in range(2):
            greet.append(at(lax.rem(zh + j, NZ), y, core, b, x))
    for device in greet:
        pl.semaphore_signal(barrier, inc=1, device_id=device, device_id_type=MESH)

    lane = lax.broadcasted_iota(jnp.int32, (1, HD), 1)
    starts = jnp.zeros((1, HD), jnp.int32)
    ends = jnp.zeros((1, HD), jnp.int32)
    total = jnp.int32(0)
    for n in range(NDOCS):
        starts = jnp.where(lane == n, total, starts)
        total = total + doc_ref[n]
        ends = jnp.where(lane == n, total, ends)
    row_of = lax.broadcasted_iota(jnp.int32, (TILE, HD), 0)
    lane_of = lax.broadcasted_iota(jnp.int32, (TILE, HD), 1)
    named = lane_of < NDOCS

    def features(n, carry):
        pos = seq * TOK + n * TILE + row_of
        inside = (pos >= starts) & (pos < ends)
        other = jnp.where(named & jnp.logical_not(inside), 1.0, 0.0).astype(jnp.bfloat16)
        for h in range(HEADS):
            qx[n, h * TILE:(h + 1) * TILE, HD:] = other
            qx[n, h * TILE:(h + 1) * TILE, :HD] = q_ref[pl.ds(pl.multiple_of(n * TILE, TILE), TILE), h * HD:(h + 1) * HD]
        for d in range(5):
            key_pos = pos - d * TOK
            hidden = ((key_pos >= starts) & (key_pos < ends)) | (key_pos < 0)
            kf[d, pl.ds(pl.multiple_of(n * TILE, TILE), TILE), :] = jnp.where(named & hidden, LOW, 0.0).astype(jnp.bfloat16)
        return carry

    lax.fori_loop(0, TOK // TILE, features, 0)

    diff = (row_of - lane_of).astype(jnp.float32)

    def weight(distance_left, ramp, seen):
        w = jnp.clip(distance_left / ramp, 0.0, 1.0)
        keep = (w > 0.0) & seen
        return jnp.where(keep, jnp.log2(jnp.where(keep, w, 1.0)), LOW)

    for h in range(HEADS):
        ramp = ramp_ref[head * HEADS + h].astype(jnp.float32)
        span = span_ref[head * HEADS + h].astype(jnp.float32) * float(TILE)
        always = diff < 1000.0
        btab[h, 0] = jnp.zeros((TILE, HD), jnp.float32)
        btab[h, 1] = weight(float(TILE) - diff, ramp, always)
        btab[h, 2] = weight(-diff, ramp, always)
        btab[h, 3] = weight(span - diff, ramp, diff >= 0.0)
        btab[h, 4] = jnp.full((TILE, HD), LOW, jnp.float32)

    pl.semaphore_wait(barrier, len(greet))

    def remote(src, dst, send, recv, device):
        return pltpu.make_async_remote_copy(
            src_ref=src, dst_ref=dst, send_sem=send, recv_sem=recv,
            device_id=device, device_id_type=MESH)

    def kv_copies(k_src, v_src, slot, n, device):
        return (remote(k_src, kbuf.at[slot], kv_send.at[n, 0], kv_recv.at[slot, 0], device),
                remote(v_src, vbuf.at[slot], kv_send.at[n, 1], kv_recv.at[slot, 1], device))

    def start(copies):
        for c in copies:
            c.start()

    def kv_arrived(slot):
        for c in kv_copies(k_ref, v_ref, slot, 0, sibling):
            c.wait_recv()

    start(kv_copies(k_ref, v_ref, 1, 0, after))

    @pl.when(core == 0)
    def _():
        start(kv_copies(k_ref, v_ref, 0, 2, sibling))

    mine = (zl, lax.rem(zh, 2))

    def z_copy(j):
        target = at(lax.rem(zh + j, NZ), y, core, half, x)
        return remote(w_ref, wg.at[mine[0], mine[1], y, core], z_send.at[j], z_recv.at[mine[0], mine[1]], target)

    for j in range(1, NZ):
        z_copy(j).start()

    @pl.when(half == zl)
    def _():
        pltpu.make_async_copy(w_ref, wg.at[mine[0], mine[1], y, core], z_recv.at[mine[0], mine[1]]).start()

    @pl.when(half != zl)
    def _():
        z_copy(0).start()

    def chunk(y_, c_):
        return wg.at[:, :, y_, c_]

    def ring_up(n):
        src = chunk(lax.rem(y + NY - n, NY), core)
        return remote(src, src, p_send.at[n], p_recv.at[n], y_up)

    def ring_down(n):
        src = chunk(lax.rem(y + n, NY), core)
        return remote(src, src, m_send.at[n], m_recv.at[n], y_down)

    def got_up(n):
        src = chunk(lax.rem(y + NY - n - 1, NY), core)
        return remote(src, src, p_send.at[n], p_recv.at[n], y_up)

    def got_down(n):
        src = chunk(lax.rem(y + n + 1, NY), core)
        return remote(src, src, m_send.at[n], m_recv.at[n], y_down)

    def share(n):
        src = chunk(lax.rem(y + n, NY), core)
        return remote(src, src, s_send.at[n], s_recv.at[n], sibling)

    def shared(n):
        src = chunk(lax.rem(y + n, NY), 1 - core)
        return remote(src, src, s_send.at[n], s_recv.at[n], sibling)

    def ring_begin():
        for a in range(2):
            for b in range(2):
                dst = wg.at[a, b, y, core]
                remote(w_ref, dst, z_send.at[0], z_recv.at[a, b], sibling).wait_recv()
        ring_down(0).start()
        ring_up(0).start()
        share(0).start()

    def ring_step(n):
        if n < MINUS:
            got_down(n).wait_recv()
            if n + 1 < MINUS:
                ring_down(n + 1).start()
            share(n + 1).start()
        if n < PLUS:
            got_up(n).wait_recv()
            if n + 1 < PLUS:
                ring_up(n + 1).start()
            share(NY - n - 1).start()

    def send_att(i):
        rows = att.at[zl, pl.ds(pl.multiple_of(i * TILE, TILE), TILE)]
        return remote(rows, rows, a_send.at[i], a_recv.at[i], partner)

    def attend(d, keys, values, last=False):
        def tile(i, carry):
            kx = jnp.concatenate([keys[...], kf[d]], axis=1)
            s_scr[...] = lax.dot_general(qx[i], kx, NT, preferred_element_type=jnp.float32)
            for h in range(HEADS):
                span = span_ref[head * HEADS + h]
                rows = slice(h * TILE, (h + 1) * TILE)
                terms = []
                for t in range(4):
                    delta = 4 * d + i - t
                    over = delta - span
                    table = jnp.where(over > 0, 4, jnp.maximum(over + 2, 0))
                    table = jnp.where(delta > 0, table, jnp.where(delta == 0, 3, 4))
                    terms.append(s_scr[rows, t * TILE:(t + 1) * TILE] * SCALE + btab[h, table])
                top = jnp.maximum(jnp.maximum(terms[0], terms[1]), jnp.maximum(terms[2], terms[3]))
                top = jnp.broadcast_to(jnp.max(top, axis=1, keepdims=True), (TILE, HD))
                if d > 0:
                    old = m_scr[i, rows, :]
                    top = jnp.maximum(old, top)
                    ratio = jnp.exp2(old - top)
                    acc[i, rows, :] = acc[i, rows, :] * jnp.concatenate([ratio, ratio], axis=1)
                m_scr[i, rows, :] = top
                for t in range(4):
                    p_scr[rows, t * TILE:(t + 1) * TILE] = jnp.exp2(terms[t] - top).astype(jnp.bfloat16)
            vx = jnp.concatenate([values[...], jnp.ones((TOK, HD), jnp.bfloat16)], axis=1)
            more = jnp.dot(p_scr[...], vx, preferred_element_type=jnp.float32)
            acc[i] = more if d == 0 else acc[i] + more
            if last:
                for h in range(HEADS):
                    rows = slice(h * TILE, (h + 1) * TILE)
                    out = acc[i, rows, :HD] / acc[i, rows, HD:]
                    att[zl, pl.ds(pl.multiple_of(i * TILE, TILE), TILE), h * HD:(h + 1) * HD] = out.astype(jnp.bfloat16)
                send_att(i).start()
            return carry

        lax.fori_loop(0, TOK // TILE, tile, 0)

    attend(0, k_ref, v_ref)
    kv_arrived(1)
    start(kv_copies(kbuf.at[1], vbuf.at[1], 3, 1, after))

    @pl.when(core == 0)
    def _():
        start(kv_copies(kbuf.at[1], vbuf.at[1], 2, 3, sibling))

    @pl.when(core == 1)
    def _():
        start(kv_copies(kbuf.at[1], vbuf.at[1], 0, 2, sibling))

    ring_begin()
    attend(2, kbuf.at[1], vbuf.at[1])
    kv_arrived(0)
    attend(1, kbuf.at[0], vbuf.at[0])
    ring_step(0)
    kv_arrived(3)

    @pl.when(core == 1)
    def _():
        start(kv_copies(kbuf.at[3], vbuf.at[3], 2, 3, sibling))

    attend(4, kbuf.at[3], vbuf.at[3])
    ring_step(1)
    kv_arrived(2)
    attend(3, kbuf.at[2], vbuf.at[2], last=True)
    ring_step(2)
    ring_step(3)

    for i in range(TOK // TILE):
        rows = att.at[1 - zl, pl.ds(i * TILE, TILE)]
        remote(rows, rows, a_send.at[i], a_recv.at[i], partner).wait_recv()
    for n in range(NY):
        shared(n).wait_recv()

    def far_copy(blk):
        return remote(part.at[blk, :, xo], far.at[blk], far_send.at[blk], far_recv.at[blk], x_up if blk < 2 else x_down)

    def near_copy(way, blk):
        return remote(part.at[blk, :, xr if way == 0 else xl], near.at[way, blk], near_send.at[way, blk],
                      near_recv.at[way, blk], x_up if way == 0 else x_down)

    def zx_copy(blk):
        return remote(zout.at[blk], zin.at[blk], zx_send.at[blk], zx_recv.at[blk], partner)

    def project(blk):
        side, low = blk // 2, (blk % 2) * (NY // 2)
        sums = jnp.zeros((TOK, COLS), jnp.float32)
        for a in range(2):
            rows = wg[a, side, low:low + NY // 2].reshape(COLS, FEAT)
            sums = sums + lax.dot_general(att[a], rows, NT, preferred_element_type=jnp.float32)
        part[blk] = sums.astype(jnp.bfloat16).reshape(2, NX, ROWS, COLS)

    order = (0, 2, 1, 3)
    for blk in order:
        project(blk)
        far_copy(blk).start()
    for blk in order:
        near_copy(1 if blk < 2 else 0, blk).start()
    for blk in order:
        far_copy(blk).wait_recv()
        way = 0 if blk < 2 else 1
        to = xr if way == 0 else xl
        part[blk, :, to] = (part[blk, :, to].astype(jnp.float32) + far[blk].astype(jnp.float32)).astype(jnp.bfloat16)
        near_copy(way, blk).start()
    for blk in order:
        for way in (1, 0) if blk < 2 else (0, 1):
            near_copy(way, blk).wait_recv()

        def whole(b):
            return (part[blk, b, x].astype(jnp.float32) + near[0, blk, b].astype(jnp.float32)
                    + near[1, blk, b].astype(jnp.float32)).astype(jnp.bfloat16)

        zout[blk] = whole(1 - zl)
        zx_copy(blk).start()
        out_ref[:, pl.ds(pl.multiple_of(zl * 4 * COLS + blk * COLS, COLS), COLS)] = whole(zl)
    for blk in order:
        zx_copy(blk).wait_recv()
        out_ref[:, pl.ds(pl.multiple_of((1 - zl) * 4 * COLS + blk * COLS, COLS), COLS)] = zin[blk]

    for c in kv_copies(k_ref, v_ref, 1, 0, after) + kv_copies(k_ref, v_ref, 3, 1, after):
        c.wait_send()
    for n in (2, 3):
        for c in kv_copies(k_ref, v_ref, 0, n, sibling):
            c.wait_send()
    for j in range(1, NZ):
        z_copy(j).wait_send()

    @pl.when(half != zl)
    def _():
        z_copy(0).wait_send()

    for n in range(PLUS):
        ring_up(n).wait_send()
    for n in range(MINUS):
        ring_down(n).wait_send()
    for n in range(NY):
        share(n).wait_send()
    for i in range(TOK // TILE):
        send_att(i).wait_send()
    for blk in order:
        far_copy(blk).wait_send()
        near_copy(0, blk).wait_send()
        near_copy(1, blk).wait_send()
        zx_copy(blk).wait_send()


def on_device(query_feats, key_feats, value_feats, span_class, ramp_width, doc_lengths, out_proj):
    bf16, f32 = jnp.bfloat16, jnp.float32
    dma = pltpu.SemaphoreType.DMA
    vmem = pl.BlockSpec(memory_space=pltpu.VMEM)
    smem = pl.BlockSpec(memory_space=pltpu.SMEM)
    return pl.pallas_call(
        kernel,
        out_shape=jax.ShapeDtypeStruct((ROWS, 8 * COLS), bf16),
        in_specs=[vmem] * 4 + [smem] * 3,
        out_specs=vmem,
        scratch_shapes=[
            pltpu.VMEM((4, TOK, HD), bf16),
            pltpu.VMEM((4, TOK, HD), bf16),
            pltpu.VMEM((4, HEADS * TILE, 2 * HD), bf16),
            pltpu.VMEM((5, TOK, HD), bf16),
            pltpu.VMEM((HEADS, 5, TILE, HD), f32),
            pltpu.VMEM((HEADS * TILE, TOK), f32),
            pltpu.VMEM((HEADS * TILE, TOK), bf16),
            pltpu.VMEM((4, HEADS * TILE, HD), f32),
            pltpu.VMEM((4, HEADS * TILE, 2 * HD), f32),
            pltpu.VMEM((2, TOK, FEAT), bf16),
            pltpu.VMEM((2, 2, NY, 2, ROWS, FEAT), bf16),
            pltpu.VMEM((4, 2, NX, ROWS, COLS), bf16),
            pltpu.VMEM((4, 2, ROWS, COLS), bf16),
            pltpu.VMEM((2, 4, 2, ROWS, COLS), bf16),
            pltpu.VMEM((4, ROWS, COLS), bf16),
            pltpu.VMEM((4, ROWS, COLS), bf16),
            dma((4, 2)), dma((4, 2)), dma((NZ,)), dma((2, 2)),
            dma((PLUS,)), dma((PLUS,)), dma((MINUS,)), dma((MINUS,)),
            dma((NY,)), dma((NY,)), dma((4,)), dma((4,)),
            dma((4,)), dma((4,)), dma((2, 4)), dma((2, 4)),
            dma((4,)), dma((4,)),
        ],
        compiler_params=pltpu.CompilerParams(
            collective_id=0, has_side_effects=True, vmem_limit_bytes=48 * 2**20),
        cost_estimate=pl.CostEstimate(flops=8 * 10**9, bytes_accessed=2 * 10**6, transcendentals=6 * 10**6),
        name="layer",
    )(query_feats, key_feats, value_feats, out_proj, span_class, ramp_width, doc_lengths)


def solution(mesh):
    split = P("seq", "head")
    return jax.shard_map(
        on_device, mesh=mesh, in_specs=(split, split, split, P(), P(), P(), split),
        out_specs=P(("seq", "head"), None), check_vma=False)
```

time: 196 us -> 101 us (0.52)
  waiting for transfers between devices: 125 us -> 0 us
  Pallas kernels: 0 us -> 94.2 us
  matrix products: 23.4 us -> 0 us
  between operations: 16.2 us -> 0.02 us
  starting transfers between devices: 15.6 us -> 0 us
  other arithmetic: 13.5 us -> 0 us
  local copies, waits for them, and re-layouts: 1.3 us -> 6.45 us
    pallas_call x0 -> x1, Pallas kernels: none -> 94.2 us  [on_device(): pl.pallas_call(kernel, out_shape=jax.ShapeDtypeStruct((ROWS, 8 * COLS), b...]
    all_gather x1 -> x0, waiting for transfers between devices: 70.6 us -> none  [on_device(): lax.all_gather(out_proj, 'seq', axis=0, tiled=True)]
    reduce_scatter x1 -> x0, waiting for transfers between devices: 53.9 us -> none  [on_device(): lax.psum_scatter(partials.astype(jnp.bfloat16), 'head', scatter_dimension...]
    dot_general x9 -> x0, matrix products: 23.4 us -> none  [the longest x4 9.32 us: attend(): jnp.einsum('qgrk,kgd->qgrd', prob_terms.astype(jnp.bfloat16), value_block...]
    ppermute x4 -> x0, starting transfers between devices: 15.6 us -> none  [shifted(): return lax.ppermute(block, axis, route)]
    reduce_sum x4 -> x0, other arithmetic: 7.53 us -> none  [attend(): denominator = denominator * rescale + jnp.sum(prob_terms, axis=3)]
    unnamed x5 -> x15, local copies, waits for them, and re-layouts: 0.23 us -> 6.45 us
  transfers between devices with their start and end apart: 6 -> 0, of which waited for: 2 -> 0; matrix products, arithmetic and copies ran while one was open for 16% -> 0% of each run, Pallas kernels for 0% -> 0%
where the time goes in v1:
time: 101 us
  Pallas kernels  94.2 us (93%)
  local copies, waits for them, and re-layouts  6.45 us (6%)
    pallas_call x1, Pallas kernels, on_device(): pl.pallas_call(kernel, out_shape=jax.ShapeDtypeStruct((ROWS, 8 * COLS), b...  94.2 us
    unnamed x15, local copies, waits for them, and re-layouts  6.45 us

profile of v1, /device:TPU:1, one launch (start us, length us, event | category | flops | bytes accessed | tf_op | source)
XLA Modules:
  0.0 100.6 jit_solution(5043761810218674611)
XLA Ops:
  0.0 0.0 copy-start
  0.0 1.0 %copy-done = bf16[512,512]{1,0:T(8,128)(2,1)S(1)} copy-done((bf16[512,512]{1,0:T(8,128)(2,1)S(1)}, bf16[512,512]{1,0:T(8,128)(2,1)}, u32[]{:S(2)}) %copy-start) | copy-done | bytes 524312
  1.0 0.0 copy-start.1
  1.0 0.9 copy-done.1
  1.9 0.0 copy-start.2
  1.9 0.9 copy-done.2
  2.9 0.0 copy-start.3
  2.9 0.8 copy-done.3
  3.7 0.0 copy-start.4
  3.7 0.7 copy-done.4
  4.3 0.0 copy-start.5
  4.3 0.7 copy-done.5
  5.0 0.0 copy-start.6
  5.0 0.7 copy-done.6
  5.7 94.2 %layer.1 = bf16[64,4096]{1,0:T(8,128)(2,1)S(1)} custom-call(bf16[512,512]{1,0:T(8,128)(2,1)S(1)} %copy-done, bf16[512,128]{1,0:T(8,128)(2,1)S(1)} %copy-done.1, bf16[512,128]{1,0:T(8,128)(2,1)S(1)} %copy-done.2, bf16[64,512]{1,0:T(8,128)(2,1)S(1)} %copy-done.3, s32[32]{0:T(128)S(1)} %copy-done.4, s32[32]{0:T(128)S(1)} %copy-done.5, s32[16]{0:T(128)S(1)} %copy-done.6), custom_call_target="tpu_custom_call" | custom-call | flops 8000000000 | bytes 2000000 | tf_op jit(solution)/shard_map/layer/pallas_call | solution.py:352
  99.8 0.8 copy.9
Async XLA Ops:
  0.0 1.0 %copy-start = (bf16[512,512]{1,0:T(8,128)(2,1)S(1)}, bf16[512,512]{1,0:T(8,128)(2,1)}, u32[]{:S(2)}) copy-start(bf16[512,512]{1,0:T(8,128)(2,1)} %q_ref.1) | copy-start | bytes 1572868
  1.0 0.9 copy-start.1
  1.9 0.9 copy-start.2
  2.9 0.8 copy-start.3
  3.7 0.7 copy-start.4
  4.3 0.7 copy-start.5
  5.0 0.7 copy-start.6

commit v2 on v1

v2 whole, which is shorter than its diff:
```python
import math

import jax
import jax.numpy as jnp
from jax import lax
from jax.experimental import pallas as pl
from jax.experimental.pallas import tpu as pltpu
from jax.sharding import PartitionSpec as P

HD = 128
TILE = 128
HEADS = 4
TOK = 512
FEAT = HEADS * HD
NZ, NY, NX = 4, 8, 4
NDOCS = 16
ROWS = 64
UP, DOWN = 2, 4
LOW = -1e30
MESH = pl.DeviceIdType.MESH
NT = (((1,), (1,)), ((), ()))
SCALE = math.log2(math.e) / math.sqrt(HD)


def kernel(q_hbm, k_hbm, v_hbm, w_hbm, span_hbm, ramp_hbm, doc_hbm, out_ref,
           q_ref, k_ref, v_ref, w_ref, span_ref, ramp_ref, doc_ref,
           kbuf, vbuf, qx, kf, btab, s_one, s_two, p_one, p_two, m_scr, acc, att, wg, part,
           far, near, zout, zin,
           khop, vhop, hop_send, hop_recv, in_sem, kv_send, kv_recv, z_send, z_recv, p_send, p_recv, m_send, m_recv,
           s_send, s_recv, a_send, a_recv, far_send, far_recv, near_send, near_recv,
           zx_send, zx_recv):
    loads = [pltpu.make_async_copy(src, dst, in_sem.at[n]) for n, (src, dst) in enumerate((
        (doc_hbm, doc_ref), (span_hbm, span_ref), (ramp_hbm, ramp_ref), (k_hbm, k_ref),
        (v_hbm, v_ref), (w_hbm, w_ref), (q_hbm, q_ref)))]
    for c in loads:
        c.start()
    s_scr, p_scr = (s_one, s_two), (p_one, p_two)
    seq = lax.axis_index("seq")
    head = lax.axis_index("head")
    core = lax.rem(seq, 2)
    y = lax.rem(seq // 2, NY)
    zh = seq // (2 * NY)
    x = lax.rem(head, NX)
    zl = head // NX
    half = zh // 2
    n_seq = 2 * NY * NZ
    chip = seq // 2
    last_chip = NY * NZ - 1
    leaves = zh < NZ - 1
    came = zh > 0

    def at(zh_, y_, c_, zl_, x_):
        return ((zh_ * NY + y_) * 2 + c_, zl_ * NX + x_)

    after = (lax.rem(seq + 2, n_seq), head)
    before = (lax.rem(seq + n_seq - 2, n_seq), head)
    sibling = at(zh, y, 1 - core, zl, x)
    y_up = at(zh, lax.rem(y + 1, NY), core, zl, x)
    y_down = at(zh, lax.rem(y + NY - 1, NY), core, zl, x)
    xr, xl = lax.rem(x + 1, NX), lax.rem(x + NX - 1, NX)
    xo = lax.rem(x + 2, NX)
    x_up = at(zh, y, core, zl, xr)
    x_down = at(zh, y, core, zl, xl)
    z_next = at(lax.rem(zh + 1, NZ), y, core, zl, x)
    partner = at(zh, y, core, 1 - zl, x)

    @pl.when(chip < 2)
    def _():
        kbuf[...] = jnp.zeros_like(kbuf)
        vbuf[...] = jnp.zeros_like(vbuf)

    barrier = pltpu.get_barrier_semaphore()
    greet = [sibling, y_up, y_down, x_up, x_down, partner]
    for j in range(1, NZ):
        for b in range(2):
            greet.append(at(lax.rem(zh + j, NZ), y, core, b, x))
    for device in greet:
        pl.semaphore_signal(barrier, inc=1, device_id=device, device_id_type=MESH)

    @pl.when(chip < last_chip)
    def _():
        pl.semaphore_signal(barrier, inc=1, device_id=after, device_id_type=MESH)

    @pl.when(chip > 0)
    def _():
        pl.semaphore_signal(barrier, inc=1, device_id=before, device_id_type=MESH)

    for c in loads:
        c.wait()

    pl.semaphore_wait(barrier, len(greet) + jnp.where(chip < last_chip, 1, 0) + jnp.where(chip > 0, 1, 0))

    def remote(src, dst, send, recv, device):
        return pltpu.make_async_remote_copy(
            src_ref=src, dst_ref=dst, send_sem=send, recv_sem=recv,
            device_id=device, device_id_type=MESH)

    def kv_copies(k_src, v_src, slot, n, device):
        return (remote(k_src, kbuf.at[slot], kv_send.at[n, 0], kv_recv.at[slot, 0], device),
                remote(v_src, vbuf.at[slot], kv_send.at[n, 1], kv_recv.at[slot, 1], device))

    def start(copies):
        for c in copies:
            c.start()

    def start_if(condition, copies):
        @pl.when(condition)
        def _():
            start(copies)

    def sent_if(condition, copies):
        @pl.when(condition)
        def _():
            for c in copies:
                c.wait_send()

    def kv_arrived(slot, condition):
        @pl.when(condition)
        def _():
            for c in kv_copies(k_ref, v_ref, slot, 0, sibling):
                c.wait_recv()

    k_on, v_on = kv_copies(k_ref, v_ref, 1, 0, after)
    k_aside = remote(kbuf.at[1], khop, hop_send.at[1], hop_recv.at[1], z_next)
    v_aside = remote(v_ref, vhop, hop_send.at[0], hop_recv.at[0], z_next)
    k_second, v_second = kv_copies(kbuf.at[1], vbuf.at[1], 3, 1, after)
    sends = dict(
        k_on=(chip < last_chip, (k_on,)),
        v_on=(y < NY - 1, (v_on,)),
        v_aside=((y == NY - 1) & leaves, (v_aside,)),
        v_after=((y == NY - 1) & came, kv_copies(khop, vhop, 1, 4, y_up)[1:]),
        v_second=((chip > 0) & (chip < last_chip), (v_second,)),
        k_second=((chip > 0) & (y < NY - 1), (k_second,)),
        k_aside=((y == NY - 1) & leaves, (k_aside,)),
        k_after=((y == NY - 1) & came, kv_copies(khop, vhop, 3, 4, y_up)[:1]),
        own_over=(core == 0, kv_copies(k_ref, v_ref, 0, 2, sibling)),
        first_over=((core == 1) & (chip > 0), kv_copies(kbuf.at[1], vbuf.at[1], 0, 2, sibling)),
        even_over=((core == 0) & (chip > 0), kv_copies(kbuf.at[1], vbuf.at[1], 2, 3, sibling)),
        odd_over=((core == 1) & (chip > 1), kv_copies(kbuf.at[3], vbuf.at[3], 2, 3, sibling)),
    )
    for name in ("k_on", "v_aside", "v_on", "own_over"):
        start_if(*sends[name])

    mine = (zl, lax.rem(zh, 2))

    def z_copy(j):
        target = at(lax.rem(zh + j, NZ), y, core, half, x)
        return remote(w_ref, wg.at[mine[0], mine[1], y, core], z_send.at[j], z_recv.at[mine[0], mine[1]], target)

    for j in range(1, NZ):
        z_copy(j).start()

    @pl.when(half == zl)
    def _():
        pltpu.make_async_copy(w_ref, wg.at[mine[0], mine[1], y, core], z_recv.at[mine[0], mine[1]]).start()

    @pl.when(half != zl)
    def _():
        z_copy(0).start()

    def chunk(n, j, c_):
        return wg.at[:, j, lax.rem(y + n, NY), c_]

    def ring_up(n, j):
        src = chunk(NY - n, j, core)
        return remote(src, src, p_send.at[n, j], p_recv.at[n, j], y_up)

    def ring_down(n, j):
        src = chunk(n, j, core)
        return remote(src, src, m_send.at[n, j], m_recv.at[n, j], y_down)

    def got_up(n, j):
        src = chunk(NY - n - 1, j, core)
        return remote(src, src, p_send.at[n, j], p_recv.at[n, j], y_up)

    def got_down(n, j):
        src = chunk(n + 1, j, core)
        return remote(src, src, m_send.at[n, j], m_recv.at[n, j], y_down)

    def share(n, j):
        src = chunk(n, j, core)
        return remote(src, src, s_send.at[n, j], s_recv.at[n, j], sibling)

    def shared(n, j):
        src = chunk(n, j, 1 - core)
        return remote(src, src, s_send.at[n, j], s_recv.at[n, j], sibling)

    def ring_begin():
        for j in range(2):
            for a in range(2):
                remote(w_ref, wg.at[a, j, y, core], z_send.at[0], z_recv.at[a, j], sibling).wait_recv()
            ring_down(0, j).start()
            ring_up(0, j).start()
            share(0, j).start()

    def ring_step(n, j):
        def down():
            got_down(n, j).wait_recv()
            if n + 1 < DOWN:
                ring_down(n + 1, j).start()
            elif n + 1 == DOWN:
                @pl.when(j == 0)
                def _():
                    ring_down(n + 1, j).start()

            share(n + 1, j).start()

        def up():
            got_up(n, j).wait_recv()
            if n + 1 < UP:
                ring_up(n + 1, j).start()
            elif n + 1 == UP:
                @pl.when(j == 1)
                def _():
                    ring_up(n + 1, j).start()

            share(NY - n - 1, j).start()

        down()
        if n < UP:
            up()
        elif n == UP:
            pl.when(j == 1)(up)

    def ring_end():
        got_down(DOWN, 0).wait_recv()
        share(DOWN + 1, 0).start()

    lane = lax.broadcasted_iota(jnp.int32, (1, HD), 1)
    starts = jnp.zeros((1, HD), jnp.int32)
    ends = jnp.zeros((1, HD), jnp.int32)
    total = jnp.int32(0)
    for n in range(NDOCS):
        starts = jnp.where(lane == n, total, starts)
        total = total + doc_ref[n]
        ends = jnp.where(lane == n, total, ends)
    row_of = lax.broadcasted_iota(jnp.int32, (TILE, HD), 0)
    lane_of = lax.broadcasted_iota(jnp.int32, (TILE, HD), 1)
    named = lane_of < NDOCS

    def features(n, carry):
        pos = seq * TOK + n * TILE + row_of
        inside = (pos >= starts) & (pos < ends)
        other = jnp.where(named & jnp.logical_not(inside), 1.0, 0.0).astype(jnp.bfloat16)
        for h in range(HEADS):
            qx[n, h * TILE:(h + 1) * TILE, HD:] = other
            qx[n, h * TILE:(h + 1) * TILE, :HD] = q_ref[pl.ds(pl.multiple_of(n * TILE, TILE), TILE), h * HD:(h + 1) * HD]
        for d in range(5):
            key_pos = pos - d * TOK
            hidden = ((key_pos >= starts) & (key_pos < ends)) | (key_pos < 0)
            kf[d, pl.ds(pl.multiple_of(n * TILE, TILE), TILE), :] = jnp.where(named & hidden, LOW, 0.0).astype(jnp.bfloat16)
        return carry

    lax.fori_loop(0, TOK // TILE, features, 0)

    diff = (row_of - lane_of).astype(jnp.float32)

    def weight(distance_left, ramp, seen):
        w = jnp.clip(distance_left / ramp, 0.0, 1.0)
        keep = (w > 0.0) & seen
        return jnp.where(keep, jnp.log2(jnp.where(keep, w, 1.0)), LOW)

    for h in range(HEADS):
        ramp = ramp_ref[head * HEADS + h].astype(jnp.float32)
        span = span_ref[head * HEADS + h].astype(jnp.float32) * float(TILE)
        always = diff < 1000.0
        btab[h, 0] = jnp.zeros((TILE, HD), jnp.float32)
        btab[h, 1] = weight(float(TILE) - diff, ramp, always)
        btab[h, 2] = weight(-diff, ramp, always)
        btab[h, 3] = weight(span - diff, ramp, diff >= 0.0)
        btab[h, 4] = jnp.full((TILE, HD), LOW, jnp.float32)

    def send_att(i):
        rows = att.at[zl, pl.ds(pl.multiple_of(i * TILE, TILE), TILE)]
        return remote(rows, rows, a_send.at[i], a_recv.at[i], partner)

    def attend(pair, d, keys, values):
        for one in range(2):
            kx = jnp.concatenate([keys[...], kf[d]], axis=1)
            s_scr[one][...] = lax.dot_general(qx[2 * pair + one], kx, NT, preferred_element_type=jnp.float32)
        for one in range(2):
            i = 2 * pair + one
            for h in range(HEADS):
                span = span_ref[head * HEADS + h]
                rows = slice(h * TILE, (h + 1) * TILE)
                terms = []
                for t in range(4):
                    delta = 4 * d + i - t
                    over = delta - span
                    table = jnp.where(over > 0, 4, jnp.maximum(over + 2, 0))
                    table = jnp.where(delta > 0, table, jnp.where(delta == 0, 3, 4))
                    terms.append(s_scr[one][rows, t * TILE:(t + 1) * TILE] * SCALE + btab[h, table])
                top = jnp.maximum(jnp.maximum(terms[0], terms[1]), jnp.maximum(terms[2], terms[3]))
                top = jnp.broadcast_to(jnp.max(top, axis=1, keepdims=True), (TILE, HD))
                if d > 0:
                    old = m_scr[i, rows, :]
                    top = jnp.maximum(old, top)
                    ratio = jnp.exp2(old - top)
                    acc[i, rows, :] = acc[i, rows, :] * jnp.concatenate([ratio, ratio], axis=1)
                m_scr[i, rows, :] = top
                for t in range(4):
                    p_scr[one][rows, t * TILE:(t + 1) * TILE] = jnp.exp2(terms[t] - top).astype(jnp.bfloat16)
            vx = jnp.concatenate([values[...], jnp.ones((TOK, HD), jnp.bfloat16)], axis=1)
            more = jnp.dot(p_scr[one][...], vx, preferred_element_type=jnp.float32)
            acc[i] = more if d == 0 else acc[i] + more

    def over_pairs(body):
        def step(pair, carry):
            body(pair)
            return carry

        lax.fori_loop(0, 2, step, 0)

    @over_pairs
    def _(pair):
        attend(pair, 0, k_ref, v_ref)

    @pl.when((y == NY - 1) & came)
    def _():
        v_aside.wait_recv()

    start_if(*sends["v_after"])
    ring_begin()
    kv_arrived(1, chip > 0)
    for name in ("k_second", "k_aside", "v_second", "even_over", "first_over"):
        start_if(*sends[name])

    @over_pairs
    def _(pair):
        attend(pair, 2, kbuf.at[1], vbuf.at[1])
        ring_step(0, pair)

    @pl.when((y == NY - 1) & came)
    def _():
        k_aside.wait_recv()

    start_if(*sends["k_after"])
    kv_arrived(0, (core == 1) | (chip > 0))

    @over_pairs
    def _(pair):
        attend(pair, 1, kbuf.at[0], vbuf.at[0])
        ring_step(1, pair)

    late = (y < 2) & came

    @pl.when(late)
    def _():
        ring_step(2, 0)
        ring_step(2, 1)

    kv_arrived(3, chip > 1)
    start_if(*sends["odd_over"])
    kv_arrived(2, (chip > 1) | ((core == 1) & (chip > 0)))

    @over_pairs
    def _(pair):
        attend(pair, 4, kbuf.at[3], vbuf.at[3])
        attend(pair, 3, kbuf.at[2], vbuf.at[2])
        for one in range(2):
            i = 2 * pair + one
            for h in range(HEADS):
                rows = slice(h * TILE, (h + 1) * TILE)
                out = acc[i, rows, :HD] / acc[i, rows, HD:]
                att[zl, pl.ds(pl.multiple_of(i * TILE, TILE), TILE), h * HD:(h + 1) * HD] = out.astype(jnp.bfloat16)
            send_att(i).start()

        @pl.when(jnp.logical_not(late))
        def _():
            ring_step(2, pair)

    for i in range(TOK // TILE):
        rows = att.at[1 - zl, pl.ds(i * TILE, TILE)]
        remote(rows, rows, a_send.at[i], a_recv.at[i], partner).wait_recv()

    pairs = ((0, 1), (7, 2), (6, 3), (4, 5))

    def far_copy(g, j):
        return remote(part.at[g, j, :, xo], far.at[g, j], far_send.at[g, j], far_recv.at[g, j], (x_up, x_down)[j])

    def near_copy(way, g, j):
        return remote(part.at[g, j, :, (xr, xl)[way]], near.at[way, g, j], near_send.at[way, g, j],
                      near_recv.at[way, g, j], (x_up, x_down)[way])

    def zx_copy(g):
        return remote(zout.at[g], zin.at[g], zx_send.at[g], zx_recv.at[g], partner)

    def project(g):
        for p, n in enumerate(pairs[g]):
            for j in range(2):
                shared(n, j).wait_recv()
            place = lax.rem(y + n, NY)
            sums = None
            for a in range(2):
                rows = wg[a, :, place].reshape(4 * ROWS, FEAT)
                more = lax.dot_general(att[a], rows, NT, preferred_element_type=jnp.float32)
                sums = more if sums is None else sums + more
            for j in range(2):
                part[g, j, :, :, :, p * TILE:(p + 1) * TILE] = sums[:, j * TILE:(j + 1) * TILE].astype(
                    jnp.bfloat16).reshape(2, NX, ROWS, TILE)
        for j in range(2):
            far_copy(g, j).start()
        for j in range(2):
            near_copy(1 - j, g, j).start()

    def pass_on(g):
        for j in range(2):
            far_copy(g, j).wait_recv()
            to = (xr, xl)[j]
            part[g, j, :, to] = (part[g, j, :, to].astype(jnp.float32) + far[g, j].astype(jnp.float32)).astype(jnp.bfloat16)
            near_copy(j, g, j).start()

    def columns(side, g, j, p):
        return pl.ds(pl.multiple_of(((side * 2 + j) * NY + lax.rem(y + pairs[g][p], NY)) * TILE, TILE), TILE)

    def finish(g):
        for j in range(2):
            for way in (1 - j, j):
                near_copy(way, g, j).wait_recv()

            def whole(b):
                return (part[g, j, b, x].astype(jnp.float32) + near[0, g, j, b].astype(jnp.float32)
                        + near[1, g, j, b].astype(jnp.float32)).astype(jnp.bfloat16)

            zout[g, j] = whole(1 - zl)
            kept = whole(zl)
            for p in range(2):
                out_ref[:, columns(zl, g, j, p)] = kept[:, p * TILE:(p + 1) * TILE]
        zx_copy(g).start()

    def place(g):
        zx_copy(g).wait_recv()
        for j in range(2):
            for p in range(2):
                out_ref[:, columns(1 - zl, g, j, p)] = zin[g, j, :, p * TILE:(p + 1) * TILE]

    project(0)
    ring_step(3, 0)
    project(1)
    pass_on(0)
    ring_step(3, 1)
    project(2)
    pass_on(1)
    ring_end()
    project(3)
    finish(0)
    pass_on(2)
    finish(1)
    pass_on(3)
    finish(2)
    place(0)
    place(1)
    finish(3)
    place(2)
    place(3)

    for condition, copies in sends.values():
        sent_if(condition, copies)
    for j in range(1, NZ):
        z_copy(j).wait_send()

    @pl.when(half != zl)
    def _():
        z_copy(0).wait_send()

    for j in range(2):
        for n in range(UP + j):
            ring_up(n, j).wait_send()
        for n in range(DOWN + 1 - j):
            ring_down(n, j).wait_send()
        for n in range(NY):
            share(n, j).wait_send()
    for i in range(TOK // TILE):
        send_att(i).wait_send()
    for g in range(4):
        for j in range(2):
            far_copy(g, j).wait_send()
            near_copy(0, g, j).wait_send()
            near_copy(1, g, j).wait_send()
        zx_copy(g).wait_send()


def on_device(query_feats, key_feats, value_feats, span_class, ramp_width, doc_lengths, out_proj):
    bf16, f32 = jnp.bfloat16, jnp.float32
    dma = pltpu.SemaphoreType.DMA
    return pl.pallas_call(
        kernel,
        out_shape=jax.ShapeDtypeStruct((ROWS, 8 * FEAT), bf16),
        in_specs=[pl.BlockSpec(memory_space=pltpu.HBM)] * 7,
        out_specs=pl.BlockSpec(memory_space=pltpu.VMEM),
        scratch_shapes=[
            pltpu.VMEM((TOK, FEAT), bf16),
            pltpu.VMEM((TOK, HD), bf16),
            pltpu.VMEM((TOK, HD), bf16),
            pltpu.VMEM((ROWS, FEAT), bf16),
            pltpu.SMEM((32,), jnp.int32),
            pltpu.SMEM((32,), jnp.int32),
            pltpu.SMEM((NDOCS,), jnp.int32),
            pltpu.VMEM((4, TOK, HD), bf16),
            pltpu.VMEM((4, TOK, HD), bf16),
            pltpu.VMEM((4, HEADS * TILE, 2 * HD), bf16),
            pltpu.VMEM((5, TOK, HD), bf16),
            pltpu.VMEM((HEADS, 5, TILE, HD), f32),
            pltpu.VMEM((HEADS * TILE, TOK), f32),
            pltpu.VMEM((HEADS * TILE, TOK), f32),
            pltpu.VMEM((HEADS * TILE, TOK), bf16),
            pltpu.VMEM((HEADS * TILE, TOK), bf16),
            pltpu.VMEM((4, HEADS * TILE, HD), f32),
            pltpu.VMEM((4, HEADS * TILE, 2 * HD), f32),
            pltpu.VMEM((2, TOK, FEAT), bf16),
            pltpu.VMEM((2, 2, NY, 2, ROWS, FEAT), bf16),
            pltpu.VMEM((4, 2, 2, NX, ROWS, 2 * TILE), bf16),
            pltpu.VMEM((4, 2, 2, ROWS, 2 * TILE), bf16),
            pltpu.VMEM((2, 4, 2, 2, ROWS, 2 * TILE), bf16),
            pltpu.VMEM((4, 2, ROWS, 2 * TILE), bf16),
            pltpu.VMEM((4, 2, ROWS, 2 * TILE), bf16),
            pltpu.VMEM((TOK, HD), bf16), pltpu.VMEM((TOK, HD), bf16), dma((2,)), dma((2,)), dma((7,)), dma((5, 2)), dma((4, 2)), dma((NZ,)), dma((2, 2)),
            dma((UP + 1, 2)), dma((UP + 1, 2)), dma((DOWN + 1, 2)), dma((DOWN + 1, 2)),
            dma((NY, 2)), dma((NY, 2)), dma((4,)), dma((4,)),
            dma((4, 2)), dma((4, 2)), dma((2, 4, 2)), dma((2, 4, 2)),
            dma((4,)), dma((4,)),
        ],
        compiler_params=pltpu.CompilerParams(
            collective_id=0, has_side_effects=True, vmem_limit_bytes=60 * 2**20),
        cost_estimate=pl.CostEstimate(flops=8 * 10**9, bytes_accessed=2 * 10**6, transcendentals=6 * 10**6),
        name="layer",
    )(query_feats, key_feats, value_feats, out_proj, span_class, ramp_width, doc_lengths)


def solution(mesh):
    split = P("seq", "head")
    return jax.shard_map(
        on_device, mesh=mesh, in_specs=(split, split, split, P(), P(), P(), split),
        out_specs=P(("seq", "head"), None), check_vma=False)
```

time: 101 us -> 87.9 us (0.87)
  the two profiles are of different devices: /device:TPU:1 before, /device:TPU:128 now
where the time goes in v2:
time: 87.9 us; the launch traced here: 87.8 us
  Pallas kernels  85.9 us (98%)
  local copies, waits for them, and re-layouts  1.87 us (2%)
    pallas_call x1, Pallas kernels, on_device(): pl.pallas_call(kernel, out_shape=jax.ShapeDtypeStruct((ROWS, 8 * FEAT), b...  85.9 us
    unnamed x1, local copies, waits for them, and re-layouts  1.87 us

profile of v2, /device:TPU:128, one launch (start us, length us, event | category | flops | bytes accessed | tf_op | source)
XLA Modules:
  0.0 87.8 jit_solution(14998796817940350193)
XLA Ops:
  0.0 85.9 %layer.1 = bf16[64,4096]{1,0:T(8,128)(2,1)} custom-call(bf16[512,512]{1,0:T(8,128)(2,1)} %q_hbm.1, bf16[512,128]{1,0:T(8,128)(2,1)} %k_hbm.1, bf16[512,128]{1,0:T(8,128)(2,1)} %v_hbm.1, bf16[64,512]{1,0:T(8,128)(2,1)} %w_hbm.1, s32[32]{0:T(128)} %span_hbm.1, s32[32]{0:T(128)} %ramp_hbm.1, s32[16]{0:T(128)} %doc_hbm.1), custom_call_target="tpu_custom_call" | custom-call | flops 8000000000 | bytes 2000000 | tf_op jit(solution)/shard_map/layer/pallas_call | solution.py:486
  85.9 1.9 %copy.9 = bf16[64,4096]{1,0:T(8,128)(2,1)} copy(bf16[64,4096]{1,0:T(8,128)(2,1)} %layer.1) | data formatting | bytes 1048576

commit v3 on v2

--- a/solution.py
+++ b/solution.py
@@ -143,23 +143,30 @@
 
     mine = (zl, lax.rem(zh, 2))
 
-    def z_copy(j):
+    def part_of(ref, r):
+        return ref.at[pl.ds(r * (ROWS // 2), ROWS // 2)]
+
+    def z_copy(j, r):
         target = at(lax.rem(zh + j, NZ), y, core, half, x)
-        return remote(w_ref, wg.at[mine[0], mine[1], y, core], z_send.at[j], z_recv.at[mine[0], mine[1]], target)
-
-    for j in range(1, NZ):
-        z_copy(j).start()
-
-    @pl.when(half == zl)
-    def _():
-        pltpu.make_async_copy(w_ref, wg.at[mine[0], mine[1], y, core], z_recv.at[mine[0], mine[1]]).start()
-
-    @pl.when(half != zl)
-    def _():
-        z_copy(0).start()
+        return remote(part_of(w_ref, r), part_of(wg.at[mine[0], mine[1], y, core], r), z_send.at[j, r],
+                      z_recv.at[mine[0], mine[1], r], target)
+
+    for r in range(2):
+        for j in range(1, NZ):
+            z_copy(j, r).start()
+
+        @pl.when(half == zl)
+        def _():
+            pltpu.make_async_copy(part_of(w_ref, r), part_of(wg.at[mine[0], mine[1], y, core], r),
+                                  z_recv.at[mine[0], mine[1], r]).start()
+
+        @pl.when(half != zl)
+        def _():
+            z_copy(0, r).start()
 
     def chunk(n, j, c_):
-        return wg.at[:, j, lax.rem(y + n, NY), c_]
+        rows = pl.ds(pl.multiple_of(j * (ROWS // 2), ROWS // 2), ROWS // 2)
+        return wg.at[:, :, lax.rem(y + n, NY), c_, rows]
 
     def ring_up(n, j):
         src = chunk(NY - n, j, core)
@@ -188,7 +195,9 @@
     def ring_begin():
         for j in range(2):
             for a in range(2):
-                remote(w_ref, wg.at[a, j, y, core], z_send.at[0], z_recv.at[a, j], sibling).wait_recv()
+                for b in range(2):
+                    remote(part_of(w_ref, j), part_of(wg.at[a, b, y, core], j), z_send.at[0, j],
+                           z_recv.at[a, b, j], sibling).wait_recv()
             ring_down(0, j).start()
             ring_up(0, j).start()
             share(0, j).start()
@@ -320,35 +329,35 @@
         v_aside.wait_recv()
 
     start_if(*sends["v_after"])
+    late = (y == 0) & came
+
+    def relay(now):
+        kv_arrived(1, now & (chip > 0))
+        for name in ("k_aside", "v_second", "k_second", "even_over", "first_over"):
+            start_if(now & sends[name][0], sends[name][1])
+
+    relay(jnp.logical_not(late))
     ring_begin()
-    kv_arrived(1, chip > 0)
-    for name in ("k_second", "k_aside", "v_second", "even_over", "first_over"):
-        start_if(*sends[name])
+    relay(late)
 
     @over_pairs
     def _(pair):
         attend(pair, 2, kbuf.at[1], vbuf.at[1])
+
+        @pl.when((pair == 1) & (y == NY - 1) & came)
+        def _():
+            k_aside.wait_recv()
+            sends["k_after"][1][0].start()
+
         ring_step(0, pair)
 
-    @pl.when((y == NY - 1) & came)
-    def _():
-        k_aside.wait_recv()
-
-    start_if(*sends["k_after"])
     kv_arrived(0, (core == 1) | (chip > 0))
 
     @over_pairs
     def _(pair):
         attend(pair, 1, kbuf.at[0], vbuf.at[0])
-        ring_step(1, pair)
-
-    late = (y < 2) & came
-
-    @pl.when(late)
-    def _():
-        ring_step(2, 0)
-        ring_step(2, 1)
-
+
+    ring_step(1, 0)
     kv_arrived(3, chip > 1)
     start_if(*sends["odd_over"])
     kv_arrived(2, (chip > 1) | ((core == 1) & (chip > 0)))
@@ -365,9 +374,13 @@
                 att[zl, pl.ds(pl.multiple_of(i * TILE, TILE), TILE), h * HD:(h + 1) * HD] = out.astype(jnp.bfloat16)
             send_att(i).start()
 
-        @pl.when(jnp.logical_not(late))
-        def _():
-            ring_step(2, pair)
+        @pl.when(pair == 0)
+        def _():
+            ring_step(1, 1)
+
+    ring_step(2, 0)
+    ring_step(2, 1)
+    ring_step(3, 0)
 
     for i in range(TOK // TILE):
         rows = att.at[1 - zl, pl.ds(i * TILE, TILE)]
@@ -435,7 +448,6 @@
                 out_ref[:, columns(1 - zl, g, j, p)] = zin[g, j, :, p * TILE:(p + 1) * TILE]
 
     project(0)
-    ring_step(3, 0)
     project(1)
     pass_on(0)
     ring_step(3, 1)
@@ -456,12 +468,13 @@
 
     for condition, copies in sends.values():
         sent_if(condition, copies)
-    for j in range(1, NZ):
-        z_copy(j).wait_send()
-
-    @pl.when(half != zl)
-    def _():
-        z_copy(0).wait_send()
+    for r in range(2):
+        for j in range(1, NZ):
+            z_copy(j, r).wait_send()
+
+        @pl.when(half != zl)
+        def _():
+            z_copy(0, r).wait_send()
 
     for j in range(2):
         for n in range(UP + j):
@@ -514,7 +527,7 @@
             pltpu.VMEM((2, 4, 2, 2, ROWS, 2 * TILE), bf16),
             pltpu.VMEM((4, 2, ROWS, 2 * TILE), bf16),
             pltpu.VMEM((4, 2, ROWS, 2 * TILE), bf16),
-            pltpu.VMEM((TOK, HD), bf16), pltpu.VMEM((TOK, HD), bf16), dma((2,)), dma((2,)), dma((7,)), dma((5, 2)), dma((4, 2)), dma((NZ,)), dma((2, 2)),
+            pltpu.VMEM((TOK, HD), bf16), pltpu.VMEM((TOK, HD), bf16), dma((2,)), dma((2,)), dma((7,)), dma((5, 2)), dma((4, 2)), dma((NZ, 2)), dma((2, 2, 2)),
             dma((UP + 1, 2)), dma((UP + 1, 2)), dma((DOWN + 1, 2)), dma((DOWN + 1, 2)),
             dma((NY, 2)), dma((NY, 2)), dma((4,)), dma((4,)),
             dma((4, 2)), dma((4, 2)), dma((2, 4, 2)), dma((2, 4, 2)),

time: 87.9 us -> 81.8 us (0.931)
  the two profiles are of different devices: /device:TPU:128 before, /device:TPU:392 now
where the time goes in v3:
time: 81.8 us; the launch traced here: 81.6 us
  Pallas kernels  79.7 us (97%)
  local copies, waits for them, and re-layouts  1.87 us (2%)
    pallas_call x1, Pallas kernels, on_device(): pl.pallas_call(kernel, out_shape=jax.ShapeDtypeStruct((ROWS, 8 * FEAT), b...  79.7 us
    unnamed x1, local copies, waits for them, and re-layouts  1.87 us

profile of v3, /device:TPU:392, one launch (start us, length us, event | category | flops | bytes accessed | tf_op | source)
XLA Modules:
  0.0 81.6 jit_solution(8317866828501100090)
XLA Ops:
  0.0 79.7 %layer.1 = bf16[64,4096]{1,0:T(8,128)(2,1)} custom-call(bf16[512,512]{1,0:T(8,128)(2,1)} %q_hbm.1, bf16[512,128]{1,0:T(8,128)(2,1)} %k_hbm.1, bf16[512,128]{1,0:T(8,128)(2,1)} %v_hbm.1, bf16[64,512]{1,0:T(8,128)(2,1)} %w_hbm.1, s32[32]{0:T(128)} %span_hbm.1, s32[32]{0:T(128)} %ramp_hbm.1, s32[16]{0:T(128)} %doc_hbm.1), custom_call_target="tpu_custom_call" | custom-call | flops 8000000000 | bytes 2000000 | tf_op jit(solution)/shard_map/layer/pallas_call | solution.py:499
  79.7 1.9 %copy.9 = bf16[64,4096]{1,0:T(8,128)(2,1)} copy(bf16[64,4096]{1,0:T(8,128)(2,1)} %layer.1) | data formatting | bytes 1048576

commit v4 on v3

--- a/solution.py
+++ b/solution.py
@@ -358,6 +358,8 @@
         attend(pair, 1, kbuf.at[0], vbuf.at[0])
 
     ring_step(1, 0)
+
+    behind = (y < 2) & came
     kv_arrived(3, chip > 1)
     start_if(*sends["odd_over"])
     kv_arrived(2, (chip > 1) | ((core == 1) & (chip > 0)))
@@ -374,9 +376,13 @@
                 att[zl, pl.ds(pl.multiple_of(i * TILE, TILE), TILE), h * HD:(h + 1) * HD] = out.astype(jnp.bfloat16)
             send_att(i).start()
 
-        @pl.when(pair == 0)
+        @pl.when((pair == 0) & jnp.logical_not(behind))
         def _():
             ring_step(1, 1)
+
+    @pl.when(behind)
+    def _():
+        ring_step(1, 1)
 
     ring_step(2, 0)
     ring_step(2, 1)

time: 81.8 us -> 81.8 us (level)
  no operation moved by 1% of the time
where the time goes in v4:
time: 81.8 us; the launch traced here: 81.6 us
  Pallas kernels  79.7 us (97%)
  local copies, waits for them, and re-layouts  1.87 us (2%)
    pallas_call x1, Pallas kernels, on_device(): pl.pallas_call(kernel, out_shape=jax.ShapeDtypeStruct((ROWS, 8 * FEAT), b...  79.7 us
    unnamed x1, local copies, waits for them, and re-layouts  1.87 us

profile of v4, /device:TPU:392, one launch (start us, length us, event | category | flops | bytes accessed | tf_op | source)
XLA Modules:
  0.0 81.6 jit_solution(4020271137389525207)
XLA Ops:
  0.0 79.7 %layer.1 = bf16[64,4096]{1,0:T(8,128)(2,1)} custom-call(bf16[512,512]{1,0:T(8,128)(2,1)} %q_hbm.1, bf16[512,128]{1,0:T(8,128)(2,1)} %k_hbm.1, bf16[512,128]{1,0:T(8,128)(2,1)} %v_hbm.1, bf16[64,512]{1,0:T(8,128)(2,1)} %w_hbm.1, s32[32]{0:T(128)} %span_hbm.1, s32[32]{0:T(128)} %ramp_hbm.1, s32[16]{0:T(128)} %doc_hbm.1), custom_call_target="tpu_custom_call" | custom-call | flops 8000000000 | bytes 2000000 | tf_op jit(solution)/shard_map/layer/pallas_call | solution.py:505
  79.7 1.9 %copy.9 = bf16[64,4096]{1,0:T(8,128)(2,1)} copy(bf16[64,4096]{1,0:T(8,128)(2,1)} %layer.1) | data formatting | bytes 1048576

commit v5 on v3

--- a/solution.py
+++ b/solution.py
@@ -413,6 +413,8 @@
                     jnp.bfloat16).reshape(2, NX, ROWS, TILE)
         for j in range(2):
             far_copy(g, j).start()
+
+    def send_near(g):
         for j in range(2):
             near_copy(1 - j, g, j).start()
 
@@ -449,16 +451,20 @@
 
     project(0)
     project(1)
+    send_near(0)
     pass_on(0)
     ring_step(3, 1)
     project(2)
     pass_on(1)
+    send_near(1)
     ring_end()
     project(3)
+    pass_on(2)
+    send_near(2)
     finish(0)
-    pass_on(2)
+    pass_on(3)
+    send_near(3)
     finish(1)
-    pass_on(3)
     finish(2)
     place(0)
     place(1)

time: 81.8 us -> 82.1 us (level)
  no operation moved by 1% of the time
where the time goes in v5:
time: 82.1 us; the launch traced here: 82 us
  Pallas kernels  80.1 us (98%)
  local copies, waits for them, and re-layouts  1.87 us (2%)
    pallas_call x1, Pallas kernels, on_device(): pl.pallas_call(kernel, out_shape=jax.ShapeDtypeStruct((ROWS, 8 * FEAT), b...  80.1 us
    unnamed x1, local copies, waits for them, and re-layouts  1.87 us

profile of v5, /device:TPU:392, one launch (start us, length us, event | category | flops | bytes accessed | tf_op | source)
XLA Modules:
  0.0 82.0 jit_solution(11028224354446435055)
XLA Ops:
  0.0 80.1 %layer.1 = bf16[64,4096]{1,0:T(8,128)(2,1)} custom-call(bf16[512,512]{1,0:T(8,128)(2,1)} %q_hbm.1, bf16[512,128]{1,0:T(8,128)(2,1)} %k_hbm.1, bf16[512,128]{1,0:T(8,128)(2,1)} %v_hbm.1, bf16[64,512]{1,0:T(8,128)(2,1)} %w_hbm.1, s32[32]{0:T(128)} %span_hbm.1, s32[32]{0:T(128)} %ramp_hbm.1, s32[16]{0:T(128)} %doc_hbm.1), custom_call_target="tpu_custom_call" | custom-call | flops 8000000000 | bytes 2000000 | tf_op jit(solution)/shard_map/layer/pallas_call | solution.py:505
  80.1 1.9 %copy.9 = bf16[64,4096]{1,0:T(8,128)(2,1)} copy(bf16[64,4096]{1,0:T(8,128)(2,1)} %layer.1) | data formatting | bytes 1048576
